TPU v7x, 512 devices: a whole 4x8x8 slice. The times are simulated.
512 devices in a mesh: ctx: 16 (over z_lo, y), basis: 32 (over z_hi, x, core).
Axes of the slice: x: 4, y: 8, z: 8 (z_hi: 4, z_lo: 2; z = z_hi * 2 + z_lo), core: 2. Of those that a mesh axis runs over, the one named last changes fastest.
Arguments:
- out_grad: bfloat16 [4608, 8192], P('ctx', 'basis'), may hold values from -6 to 6
- inputs: bfloat16 [4608, 8192], P('ctx', 'basis'), may hold values from -6 to 6
- basis_out: bfloat16 [8192, 4096], P(None, 'basis'), may hold values from -0.0625 to 0.0625
- basis_in: bfloat16 [8192, 4096], P(None, 'basis'), may hold values from -0.0625 to 0.0625
- correction: float32 [4096, 4096], P('basis', 'ctx'), may hold values from 0.5 to 2
Outputs:
- updated: float32 [4096, 4096], P('basis', 'ctx')
All inputs are finite; a program needn't handle non-finite values.
Results may differ from a plain program's by a relative error of at most 0.0032.
Values may be sent and summed in bfloat16 or wider, within the bound.
A program may use at most 64 MiB of HBM per device.

v0:
```python
import jax
import jax.numpy as jnp
from jax import lax
from jax.sharding import PartitionSpec as P

GROUPS = 2


def body(out_grad, inputs, basis_out, basis_in, correction):
    n_basis = lax.axis_size("basis")
    n_ctx = lax.axis_size("ctx")
    tokens_here = out_grad.shape[0]
    kg_local = basis_out.shape[1]
    ka_local = basis_in.shape[1]
    ka_total = ka_local * n_basis
    half = tokens_here // GROUPS
    grad_piece = lax.all_gather(out_grad, "basis", axis=1, tiled=True)
    input_piece = lax.all_gather(inputs, "basis", axis=1, tiled=True)
    grad_rot = jnp.dot(grad_piece, basis_out, preferred_element_type=jnp.float32)
    input_rot = jnp.dot(input_piece, basis_in, preferred_element_type=jnp.float32)
    grad_rot = grad_rot.astype(jnp.bfloat16)
    input_rot = input_rot.astype(jnp.bfloat16)
    input_all = lax.all_gather(input_rot, "basis", axis=1, tiled=True)
    grad_blocks = grad_rot.reshape(GROUPS, half, kg_local)
    columns = input_all.reshape(GROUPS, half, ka_total // n_ctx * lax.axis_size("ctx"))
    product = jnp.einsum("ctk,ctg->kcg", columns, grad_blocks, preferred_element_type=jnp.float32)
    summed = lax.psum_scatter(
        product.reshape(ka_total // n_ctx * lax.axis_size("ctx"), GROUPS * kg_local),
        "ctx",
        scatter_dimension=0,
        tiled=True,
    )
    summed = summed.reshape(-1, GROUPS, kg_local)
    squared = jnp.sum(summed * summed, axis=1).T
    total_tokens = tokens_here * n_ctx
    return correction + squared / total_tokens


def solution(mesh):
    return jax.shard_map(
        body,
        mesh=mesh,
        in_specs=(
            P("ctx", "basis"),
            P("ctx", "basis"),
            P(None, "basis"),
            P(None, "basis"),
            P("basis", "ctx"),
        ),
        out_specs=P("basis", "ctx"),
        check_vma=False,
    )
```

profile of v0, /device:TPU:6, one launch (start us, length us, event | category | flops | bytes accessed | tf_op | source)
XLA Modules:
  0.0 320.6 jit_solution(15450903506109445178)
XLA Ops:
  6.5 0.0 copy-start
  6.5 0.0 all-gather.6.cloned.1.call-start
  6.5 0.7 all-gather.6.cloned.1.call-update
  7.3 0.0 all-gather.4.cloned.1.call-start
  7.3 0.7 all-gather.4.cloned.1.call-update
  8.0 0.0 all-gather.8.cloned.1.call-start
  8.1 80.8 %all-gather.6.cloned.1.call-done = bf16[288,8192]{1,0:T(8,128)(2,1)} async-done(((bf16[288,256]{1,0:T(8,128)(2,1)}), bf16[288,8192]{1,0:T(8,128)(2,1)}) %all-gather.6.cloned.1.call-update) | async-done | bytes 4718608 | tf_op jit(solution)/shard_map/all_gather | solution.py:18
  88.9 0.0 copy-done
  88.9 4.4 %convolution_convert_fusion = bf16[288,128]{1,0:T(8,128)(2,1)} fusion(bf16[288,8192]{1,0:T(8,128)(2,1)} %all-gather.6.cloned.1.call-done, bf16[8192,128]{1,0:T(8,128)(2,1)S(1)} %copy-done), kind=kOutput, calls=%fused_computation | convolution fusion | flops 604016640 | bytes 6889472 | tf_op jit(solution)/shard_map/dot_general | solution.py:20
  93.2 0.0 all-gather.8.cloned.1.call-update
  93.3 0.0 reduce-scatter.2.cloned.1.call-start
  93.3 70.4 %all-gather.4.cloned.1.call-done = bf16[288,8192]{1,0:T(8,128)(2,1)} async-done(((bf16[288,256]{1,0:T(8,128)(2,1)}), bf16[288,8192]{1,0:T(8,128)(2,1)}) %all-gather.4.cloned.1.call-update) | async-done | bytes 4718608 | tf_op jit(solution)/shard_map/all_gather | solution.py:17
  163.7 4.4 %convolution_convert_fusion.1 = bf16[288,128]{1,0:T(8,128)(2,1)S(1)} fusion(bf16[288,8192]{1,0:T(8,128)(2,1)} %all-gather.4.cloned.1.call-done, bf16[8192,128]{1,0:T(8,128)(2,1)} %param.7), kind=kOutput, calls=%fused_computation.1 | convolution fusion | flops 604016640 | bytes 6889472 | tf_op jit(solution)/shard_map/dot_general | solution.py:19
  168.2 58.5 %all-gather.8.cloned.1.call-done = bf16[288,4096]{1,0:T(8,128)(2,1)} async-done(((bf16[288,128]{1,0:T(8,128)(2,1)}), bf16[288,4096]{1,0:T(8,128)(2,1)}) %all-gather.8.cloned.1.call-update) | async-done | bytes 2359312 | tf_op jit(solution)/shard_map/all_gather | solution.py:23
  226.7 4.3 %fusion = f32[2,128,4096]{2,1,0:T(8,128)} fusion(bf16[2,144,128]{2,1,0:T(8,128)(2,1)S(1)} %bitcast.17, bf16[2,144,4096]{2,1,0:T(8,128)(2,1)} %bitcast.15), kind=kOutput, calls=%fused_computation.3 | convolution fusion | flops 301989888 | bytes 6627328 | tf_op jit(solution)/shard_map/ctk,ctg->kcg/dot_general | solution.py:26
  231.0 0.0 copy-start.1
  231.0 0.0 reduce-scatter.2.cloned.1.call-update
  231.1 81.2 %reduce-scatter.2.cloned.1.call-done = f32[256,256]{0,1:T(8,128)} async-done(((f32[4096,256]{0,1:T(8,128)}), f32[256,256]{0,1:T(8,128)}) %reduce-scatter.2.cloned.1.call-update) | async-done | bytes 262160 | tf_op jit(solution)/shard_map/reduce_scatter | solution.py:27
  312.3 1.1 mul.6
  313.4 0.0 copy-done.1
  313.4 0.7 bitcast_add_fusion
  (1 shorter events, 0.0 us)
Async XLA Ops:
  6.5 82.4 %copy-start = (bf16[8192,128]{1,0:T(8,128)(2,1)S(1)}, bf16[8192,128]{1,0:T(8,128)(2,1)}, u32[]{:S(2)}) copy-start(bf16[8192,128]{1,0:T(8,128)(2,1)} %param.8) | copy-start | bytes 6291460
  6.5 82.4 %all-gather.6.cloned.1.call-start = ((), (), s32[]{:S(2)}) async-start(), calls=%async_computation.2 | async-start | bytes 4866048 | tf_op jit(solution)/shard_map/all_gather | solution.py:18
  7.3 156.5 %all-gather.4.cloned.1.call-start = ((), (), s32[]{:S(2)}) async-start(), calls=%async_computation.1 | async-start | bytes 4866048 | tf_op jit(solution)/shard_map/all_gather | solution.py:17
  8.0 218.7 %all-gather.8.cloned.1.call-start = ((), (), s32[]{:S(2)}) async-start(), calls=%async_computation.3 | async-start | bytes 2433024 | tf_op jit(solution)/shard_map/all_gather | solution.py:23
  93.3 219.0 %reduce-scatter.2.cloned.1.call-start = ((), (), s32[]{:S(2)}) async-start(), calls=%async_computation.4 | async-start | bytes 4456448 | tf_op jit(solution)/shard_map/reduce_scatter | solution.py:27
  231.0 82.3 %copy-start.1 = (f32[128,256]{1,0:T(8,128)S(1)}, f32[128,256]{1,0:T(8,128)}, u32[]{:S(2)}) copy-start(f32[128,256]{1,0:T(8,128)} %param.9) | copy-start | bytes 393220
Sparse Core Ops, SparseCore 0:
  10.4 78.4 all-gather.5
  91.9 71.7 all-gather.3
  166.8 59.8 all-gather.7
  231.2 81.0 reduce-scatter.1
where the time goes:
time: 321 us
  waiting for transfers between devices  292 us (91%)
  between operations  13.2 us (4%)
  matrix products  13.1 us (4%)
    reduce_scatter x1, waiting for transfers between devices, body(): lax.psum_scatter(product.reshape(ka_total // n_ctx * lax.axis_size('ctx')...  81.2 us
    all_gather x1, waiting for transfers between devices, body(): input_piece = lax.all_gather(inputs, 'basis', axis=1, tiled=True)  80.8 us
    all_gather x1, waiting for transfers between devices, body(): grad_piece = lax.all_gather(out_grad, 'basis', axis=1, tiled=True)  70.4 us
    all_gather x1, waiting for transfers between devices, body(): input_all = lax.all_gather(input_rot, 'basis', axis=1, tiled=True)  58.5 us
  transfers between devices with their start and end apart: 4, of which 4 were waited for; matrix products, arithmetic and copies ran while one was open for 3% of the time, Pallas kernels for 0%

commit v1 on v0

v1 whole, which is shorter than its diff:
```python
import functools

import jax
import jax.numpy as jnp
from jax import lax
from jax.experimental import pallas as pl
from jax.experimental.pallas import tpu as pltpu
from jax.sharding import PartitionSpec as P

MESH = pl.DeviceIdType.MESH
GROUPS = 2
CHIPS = 16
CHUNKS = ((0, 80), (80, 64))
N_SEMS = 320
F32 = jnp.float32
BF16 = jnp.bfloat16


def kernel(n_tokens, grad_hbm, in_hbm, bo_hbm, bi_hbm, corr_ref, out_ref, *scratch):
    n_chunks = len(CHUNKS)
    (bo_v, bi_v, sq, sq_in, rot, ssem, rsem, asem, lsem), rest = scratch[:9], scratch[9:]
    x_land, part, part_in, a_ga = rest[:2 * n_chunks], rest[2 * n_chunks:4 * n_chunks], rest[4 * n_chunks:6 * n_chunks], rest[6 * n_chunks:7 * n_chunks]
    a_all, g_all = rest[7 * n_chunks:8 * n_chunks], rest[8 * n_chunks:9 * n_chunks]

    ctx = lax.axis_index("ctx")
    basis = lax.axis_index("basis")
    y, zl = lax.rem(ctx, 8), lax.div(ctx, 8)
    core = lax.rem(basis, 2)
    chip = lax.div(basis, 2)
    x, zh = lax.rem(chip, 4), lax.div(chip, 4)

    def wrap(v, n):
        return lax.rem(v + n, n)

    def chip_of(dz, dx):
        return wrap(zh - dz, 4) * 4 + wrap(x - dx, 4)

    def at_chip(p, k=None):
        return {"ctx": ctx, "basis": p * 2 + (core if k is None else k)}

    def at_ctx(c):
        return {"ctx": c, "basis": basis}

    sibling = at_chip(chip, 1 - core)
    x_up, x_dn = at_chip(chip_of(0, -1)), at_chip(chip_of(0, 1))
    z_up, z_dn = at_chip(chip_of(-1, 0)), at_chip(chip_of(1, 0))
    ctx_at = lambda dy, dz: wrap(zl + dz, 2) * 8 + wrap(y + dy, 8)

    barrier = pltpu.get_barrier_semaphore()
    others = [sibling, x_up, x_dn, z_up, z_dn] + [at_ctx(lax.rem(ctx + r, 16)) for r in range(1, 16)]
    for other in others:
        pl.semaphore_signal(barrier, inc=1, device_id=other, device_id_type=MESH)

    n_sem = [0]
    n_local = [0]
    started = []

    def local(src, dst):
        copy = pltpu.make_async_copy(src, dst, lsem.at[n_local[0]])
        n_local[0] += 1
        copy.start()
        return copy

    def remote(src, dst, device):
        i = n_sem[0]
        n_sem[0] += 1
        copy = pltpu.make_async_remote_copy(
            src_ref=src, dst_ref=dst, send_sem=ssem.at[i], recv_sem=rsem.at[i], device_id=device, device_id_type=MESH
        )
        copy.start()
        started.append(copy)
        return copy

    cols = pl.ds(pl.multiple_of(core * 128, 128), 128)
    b_copies = {}
    for name, hbm, v in (("a", bi_hbm, bi_v), ("g", bo_hbm, bo_v)):
        b_copies[name] = [local(hbm.at[:, core], v.at[:, :, cols])]
    own_copies = []
    for q in range(2 * n_chunks):
        src = (in_hbm, grad_hbm)[q // n_chunks]
        first, n = CHUNKS[q % n_chunks]
        own_copies.append(local(src.at[:, pl.ds(first, n)], x_land[q].at[chip]))

    pl.semaphore_wait(barrier, len(others))

    def gather(own, land, odd, got=lambda dz, dx: None):
        def slot(dz, dx):
            return land.at[chip_of(dz, dx)]

        mine = own if own is not None else slot(0, 0)
        home = slot(0, 0)
        zs = [remote(mine, home, z_up), remote(mine, home, z_dn)]
        yield
        xs = {0: [remote(mine, home, x_up), remote(mine, home, x_dn)]}
        got(0, 0)
        yield
        zs[0].wait_recv()
        zs[1].wait_recv()
        fz = remote(slot(-1, 0), slot(-1, 0), z_dn) if odd else remote(slot(1, 0), slot(1, 0), z_up)
        for dz in (1, -1):
            xs[dz] = [remote(slot(dz, 0), slot(dz, 0), x_up), remote(slot(dz, 0), slot(dz, 0), x_dn)]
        for dz in (1, -1):
            got(dz, 0)
        yield
        fz.wait_recv()
        xs[2] = [remote(slot(2, 0), slot(2, 0), x_up), remote(slot(2, 0), slot(2, 0), x_dn)]
        got(2, 0)
        yield
        fx = {}
        for i, dz in enumerate((0, 1, -1, 2)):
            xs[dz][0].wait_recv()
            xs[dz][1].wait_recv()
            if i % 2:
                fx[dz] = remote(slot(dz, -1), slot(dz, -1), x_dn)
            else:
                fx[dz] = remote(slot(dz, 1), slot(dz, 1), x_up)
            got(dz, 1)
            got(dz, -1)
        yield
        for dz in (0, 1, -1, 2):
            fx[dz].wait_recv()
            got(dz, 2)
        yield

    a_sent = []

    def spread_a(j):
        def got(dz, dx):
            owner = chip_of(dz, dx)
            i = len(a_sent)
            copy = pltpu.make_async_remote_copy(
                src_ref=a_ga[j].at[owner], dst_ref=a_all[j].at[ctx], send_sem=asem.at[i], recv_sem=asem.at[32 * n_chunks + j * 16 + ctx],
                device_id=at_ctx(owner), device_id_type=MESH,
            )
            keep = pltpu.make_async_copy(a_ga[j].at[owner], a_all[j].at[ctx], asem.at[i])
            pl.when(owner != ctx)(copy.start)
            pl.when(owner == ctx)(keep.start)
            a_sent.append((owner, copy, keep))

        return gather(None, a_ga[j], j % 2 == 1, got)

    def spread_g(j):
        up, dn = at_ctx(ctx_at(1, 0)), at_ctx(ctx_at(-1, 0))

        def slot(dy, dz):
            return g_all[j].at[ctx_at(-dy, dz)]

        over = remote(slot(0, 0), slot(0, 0), at_ctx(ctx_at(0, 1)))
        far = (4, 3) if j % 2 else (3, 4)
        ups, dns = {}, {}
        ups[1, 0], dns[1, 0] = remote(slot(0, 0), slot(0, 0), up), remote(slot(0, 0), slot(0, 0), dn)
        over.wait_recv()
        ups[1, 1], dns[1, 1] = remote(slot(0, 1), slot(0, 1), up), remote(slot(0, 1), slot(0, 1), dn)
        yield
        for hop in range(1, 5):
            for dz in (0, 1):
                if hop <= far[0]:
                    ups[hop, dz].wait_recv()
                    if hop < far[0]:
                        ups[hop + 1, dz] = remote(slot(hop, dz), slot(hop, dz), up)
                if hop <= far[1]:
                    dns[hop, dz].wait_recv()
                    if hop < far[1]:
                        dns[hop + 1, dz] = remote(slot(-hop, dz), slot(-hop, dz), dn)
            yield

    swaps = {}

    def rotate(q):
        name = "ag"[q // n_chunks]
        v = (bi_v, bo_v)[q // n_chunks]
        if q % n_chunks == 0:
            b_copies[name][0].wait()
            b_copies[name][1].wait_recv()
        own_copies[q].wait()
        n = CHUNKS[q % n_chunks][1]

        def add(s, total):
            return total + jnp.dot(x_land[q][s].reshape(2 * n, 256), v[s], preferred_element_type=F32)

        total = lax.fori_loop(0, CHIPS, add, jnp.zeros((2 * n, 256), F32))
        part[q][...] = total.reshape(2, n, 256)
        swaps[q] = remote(part[q].at[1 - core], part_in[q], sibling)

    def settle(q):
        j = q % n_chunks
        swaps[q].wait_recv()
        value = (part[q][core] + part_in[q][...]).astype(BF16)
        if q < n_chunks:
            a_ga[j][chip] = value
            return spread_a(j)
        g_all[j][ctx] = value
        return spread_g(j)

    n_q = 2 * n_chunks
    gens = []
    for q in range(n_q):
        src = (in_hbm, grad_hbm)[q // n_chunks]
        first, n = CHUNKS[q % n_chunks]
        gens.append(gather(src.at[:, pl.ds(first, n)], x_land[q], q % 2 == 1))

    def step(g):
        return next(g, "end") != "end"

    step(gens[0])
    step(gens[0])
    for name, hbm, v in (("a", bi_hbm, bi_v), ("g", bo_hbm, bo_v)):
        b_copies[name].append(remote(hbm.at[:, 1 - core], v.at[:, :, cols], sibling))
    side = []

    def advance():
        for g in list(side):
            if not step(g):
                side.remove(g)

    for q in range(n_q):
        step(gens[q])
        if q:
            step(gens[q - 1])
            rotate(q - 1)
        step(gens[q])
        if q + 1 < n_q:
            step(gens[q + 1])
        advance()
        if q:
            side.append(settle(q - 1))
            advance()
        step(gens[q])
        if q + 1 < n_q:
            step(gens[q + 1])
        advance()
        advance()
    step(gens[n_q - 1])
    rotate(n_q - 1)
    side.append(settle(n_q - 1))
    while side:
        advance()

    for owner, copy, keep in a_sent:
        pl.when(owner != ctx)(copy.wait_send)
        pl.when(owner == ctx)(keep.wait)
    rot[...] = jnp.zeros((256, 256), F32)
    for j in range(n_chunks):
        n = CHUNKS[j][1]
        for r in range(1, 16):
            c = lax.rem(ctx + r, 16)
            pltpu.make_async_copy(a_all[j].at[c], a_all[j].at[c], asem.at[32 * n_chunks + j * 16 + c]).wait()

        def multiply(i, _):
            some = pl.ds(i * 4, 4)
            left = g_all[j][some].reshape(4 * n, 256)
            right = a_all[j][some].reshape(4 * n, 256)
            rot[...] += lax.dot_general(left, right, (((0,), (0,)), ((), ())), preferred_element_type=F32)
            return 0

        lax.fori_loop(0, 4, multiply, 0)
    sq[0] = rot[:128] * rot[:128]
    sq[1] = rot[128:] * rot[128:]
    last = remote(sq.at[1 - core], sq_in, sibling)
    last.wait_recv()
    out_ref[...] = corr_ref[...] + (sq[core] + sq_in[...]) / n_tokens
    for copy in started:
        copy.wait_send()


def body(out_grad, inputs, basis_out, basis_in, correction):
    tokens = out_grad.shape[0]
    half = tokens // GROUPS
    any_ = pl.BlockSpec(memory_space=pl.ANY)
    vmem = pl.BlockSpec(memory_space=pltpu.VMEM)
    n_chunks = len(CHUNKS)
    sizes = [n for _, n in CHUNKS]
    scratch = [
        pltpu.VMEM((CHIPS, 256, 256), BF16),
        pltpu.VMEM((CHIPS, 256, 256), BF16),
        pltpu.VMEM((2, 128, 256), F32),
        pltpu.VMEM((128, 256), F32),
        pltpu.VMEM((256, 256), F32),
        pltpu.SemaphoreType.DMA((N_SEMS,)),
        pltpu.SemaphoreType.DMA((N_SEMS,)),
        pltpu.SemaphoreType.DMA((48 * n_chunks,)),
        pltpu.SemaphoreType.DMA((2 + 2 * n_chunks,)),
    ]
    scratch += [pltpu.VMEM((CHIPS, GROUPS, n, 256), BF16) for n in sizes * 2]
    scratch += [pltpu.VMEM((GROUPS, n, 256), F32) for n in sizes * 2]
    scratch += [pltpu.VMEM((n, 256), F32) for n in sizes * 2]
    scratch += [pltpu.VMEM((16, n, 256), BF16) for n in sizes * 3]
    return pl.pallas_call(
        functools.partial(kernel, tokens * lax.axis_size("ctx")),
        name="ekfac",
        out_shape=jax.ShapeDtypeStruct(correction.shape, F32),
        in_specs=[any_] * 4 + [vmem],
        out_specs=vmem,
        scratch_shapes=scratch,
        compiler_params=pltpu.CompilerParams(collective_id=0, has_side_effects=True, vmem_limit_bytes=48 << 20),
        cost_estimate=pl.CostEstimate(flops=3 * 10**9, bytes_accessed=5 * 10**6, transcendentals=0),
    )(
        out_grad.reshape(GROUPS, half, 256),
        inputs.reshape(GROUPS, half, 256),
        basis_out.reshape(CHIPS, 2, 256, 128),
        basis_in.reshape(CHIPS, 2, 256, 128),
        correction,
    )


def solution(mesh):
    return jax.shard_map(
        body,
        mesh=mesh,
        in_specs=(P("ctx", "basis"), P("ctx", "basis"), P(None, "basis"), P(None, "basis"), P("basis", "ctx")),
        out_specs=P("basis", "ctx"),
        check_vma=False,
    )
```

time: 321 us -> 129 us (0.40)
  the two profiles are of different devices: /device:TPU:6 before, /device:TPU:1 now
where the time goes in v1:
time: 129 us
  Pallas kernels  122 us (95%)
  local copies, waits for them, and re-layouts  6.56 us (5%)
    pallas_call x1, Pallas kernels, body(): pl.pallas_call(functools.partial(kernel, tokens * lax.axis_size('ctx')),...  122 us
    unnamed x11, local copies, waits for them, and re-layouts  6.56 us

profile of v1, /device:TPU:1, one launch (start us, length us, event | category | flops | bytes accessed | tf_op | source)
XLA Modules:
  0.0 128.5 jit_solution(3410091321993805898)
XLA Ops:
  0.0 0.0 copy-start
  0.0 1.6 %copy-done = bf16[8192,128]{1,0:T(8,128)(2,1)S(1)} copy-done((bf16[8192,128]{1,0:T(8,128)(2,1)S(1)}, bf16[8192,128]{1,0:T(8,128)(2,1)}, u32[]{:S(2)}) %copy-start) | copy-done | bytes 2097176
  1.6 0.0 copy-start.1
  1.6 1.6 %copy-done.1 = bf16[8192,128]{1,0:T(8,128)(2,1)S(1)} copy-done((bf16[8192,128]{1,0:T(8,128)(2,1)S(1)}, bf16[8192,128]{1,0:T(8,128)(2,1)}, u32[]{:S(2)}) %copy-start.1) | copy-done | bytes 2097176
  3.2 0.0 copy-start.2
  3.2 0.9 copy-done.2
  4.1 0.0 copy-start.3
  4.1 0.9 copy-done.3
  5.0 0.0 copy-start.4
  5.0 0.9 copy-done.4
  5.9 122.0 %ekfac.1 = f32[128,256]{1,0:T(8,128)S(1)} custom-call(bf16[2,144,256]{2,1,0:T(8,128)(2,1)S(1)} %bitcast.6, bf16[2,144,256]{2,1,0:T(8,128)(2,1)S(1)} %bitcast.7, bf16[16,2,256,128]{3,2,1,0:T(8,128)(2,1)S(1)} %bitcast.4, bf16[16,2,256,128]{3,2,1,0:T(8,128)(2,1)S(1)} %bitcast.5, f32[128,256]{1,0:T(8,128)S(1)} %copy-done.4), custom_call_target="tpu_custom_call" | custom-call | flops 3000000000 | bytes 5000000 | tf_op jit(solution)/shard_map/ekfac/pallas_call | solution.py:288
  127.9 0.7 copy.7
Async XLA Ops:
  0.0 1.6 %copy-start = (bf16[8192,128]{1,0:T(8,128)(2,1)S(1)}, bf16[8192,128]{1,0:T(8,128)(2,1)}, u32[]{:S(2)}) copy-start(bf16[8192,128]{1,0:T(8,128)(2,1)} %param.7) | copy-start | bytes 6291460
  1.6 1.6 %copy-start.1 = (bf16[8192,128]{1,0:T(8,128)(2,1)S(1)}, bf16[8192,128]{1,0:T(8,128)(2,1)}, u32[]{:S(2)}) copy-start(bf16[8192,128]{1,0:T(8,128)(2,1)} %param.8) | copy-start | bytes 6291460
  3.2 0.9 copy-start.2
  4.1 0.9 copy-start.3
  5.0 0.9 copy-start.4

commit v2 on v0

v2 whole, which is shorter than its diff:
```python
import jax
import jax.numpy as jnp
from jax import lax
from jax.experimental import pallas as pl
from jax.experimental.pallas import tpu as pltpu
from jax.sharding import PartitionSpec as P

MESH = pl.DeviceIdType.MESH
GROUPS = 2
CHIPS = 16
CHUNKS = ((0, 80), (80, 64))
N_SEMS = 90
F32 = jnp.float32
BF16 = jnp.bfloat16


def schedule(n):
    h = n // 2
    done = {}
    steps = []

    def add(op, q, upto=None):
        if 0 <= q < (h if op in "mg" else n):
            while upto is None or done.get((op, q), 0) < upto:
                steps.append((op, q))
                done[op, q] = done.get((op, q), 0) + 1
                if upto is None:
                    break

    add("x", 0, 2)
    add("x", 1, 1)
    steps.append(("b", 0))
    for q in range(n + 1):
        add("x", q, 3)
        add("x", q - 1, 6)
        add("r", q - 1)
        add("x", q, 4)
        add("x", q + 1, 1)
        add("m", q - 2, 3)
        add("s", q - 1)
        add("m", q - 1, 2)
        add("g", q - 1 - h, 1)
        add("m", q - 2, 4)
        add("x", q, 5)
        add("x", q + 1, 2)
        add("m", q - 2, 6)
        add("m", q - 1, 3)
        add("g", q - 2 - h, 9)
    return steps + [("m", j) for j in range(h) for _ in range(7 - done["m", j])] + [("g", j) for j in range(h) for _ in range(6)]


def kernel(grad_hbm, in_hbm, bo_hbm, bi_hbm, out_ref, *scratch):
    n_chunks = len(CHUNKS)
    n_q = 2 * n_chunks
    (bo_v, bi_v, sq, sq_in, rot, rot_in, sems), rest = scratch[:7], scratch[7:]
    x_land, part, part_in = rest[:n_q], rest[n_q:2 * n_q], rest[2 * n_q:3 * n_q]
    a_ga, a_all, g_all = (rest[3 * n_q + i * n_chunks:3 * n_q + (i + 1) * n_chunks] for i in range(3))

    ctx = lax.axis_index("ctx")
    basis = lax.axis_index("basis")
    y, zl = lax.rem(ctx, 8), lax.div(ctx, 8)
    core = lax.rem(basis, 2)
    chip = lax.div(basis, 2)
    x, zh = lax.rem(chip, 4), lax.div(chip, 4)

    def wrap(v, n):
        return lax.rem(v + n, n)

    def chip_of(dz, dx):
        return wrap(zh - dz, 4) * 4 + wrap(x - dx, 4)

    def at_chip(p, k):
        return {"ctx": ctx, "basis": p * 2 + k}

    def at_ctx(c):
        return {"ctx": c, "basis": basis}

    def ctx_of(dy, dz):
        return wrap(zl - dz, 2) * 8 + wrap(y - dy, 8)

    sibling = at_chip(chip, 1 - core)
    x_up, x_dn = at_chip(chip_of(0, -1), core), at_chip(chip_of(0, 1), core)
    z_up, z_dn = at_chip(chip_of(-1, 0), core), at_chip(chip_of(1, 0), core)
    peers = [at_ctx(ctx_of(-r, 0)) for r in range(1, 8)]
    over = at_ctx(ctx_of(0, 1))

    barrier = pltpu.get_barrier_semaphore()
    others = [sibling, over, x_up, x_dn, z_up, z_dn] + peers
    for other in others:
        pl.semaphore_signal(barrier, inc=1, device_id=other, device_id_type=MESH)

    used = [0]
    at_end = []

    def new():
        used[0] += 1
        return sems.at[used[0] - 1]

    def take(sem, ref):
        pltpu.make_async_copy(ref, ref, sem).wait()

    def local(src, dst):
        copy = pltpu.make_async_copy(src, dst, new())
        copy.start()
        return copy

    def remote(src, dst, device, send, recv):
        copy = pltpu.make_async_remote_copy(
            src_ref=src, dst_ref=dst, send_sem=send, recv_sem=recv, device_id=device, device_id_type=MESH
        )
        copy.start()
        return copy

    def swap(src, dst):
        copy = remote(src, dst, sibling, new(), new())
        at_end.append(copy.wait_send)
        return copy

    cols = pl.ds(pl.multiple_of(core * 128, 128), 128)
    b_copies = [[local(hbm.at[:, core], v.at[:, :, cols])] for hbm, v in ((bi_hbm, bi_v), (bo_hbm, bo_v))]
    shards, own_copies = [], []
    for q in range(n_q):
        first, n = CHUNKS[q % n_chunks]
        shards.append((in_hbm, grad_hbm)[q // n_chunks].at[:, pl.ds(first, n)])
        own_copies.append(local(shards[q], x_land[q].at[chip]))

    pl.semaphore_wait(barrier, len(others))

    def gather(own, land, odd, got=lambda dz, dx: None):
        send, z1, z2, x2 = (new() for _ in range(4))
        x1 = {dz: new() for dz in (0, 1, -1, 2)}

        def slot(dz, dx):
            return land.at[chip_of(dz, dx)]

        def hop(dz, dx, device, recv, src=None, part=None):
            dst = slot(dz, dx)
            if part is not None:
                dst = dst.at[part]
            remote(dst if src is None else src, dst, device, send, recv)

        hop(0, 0, z_up, z1, own)
        hop(0, 0, z_dn, z1, own)
        yield
        hop(0, 0, x_up, x1[0], own)
        hop(0, 0, x_dn, x1[0], own)
        got(0, 0)
        yield
        take(z1, land.at[pl.ds(0, 2)])
        if land.ndim == 4:
            hop(1, 0, z_up, z2, part=0)
            hop(-1, 0, z_dn, z2, part=1)
        elif odd:
            hop(-1, 0, z_dn, z2)
        else:
            hop(1, 0, z_up, z2)
        for dz in (1, -1):
            hop(dz, 0, x_up, x1[dz])
            hop(dz, 0, x_dn, x1[dz])
        got(1, 0)
        got(-1, 0)
        yield
        take(z2, land.at[0])
        hop(2, 0, x_up, x1[2])
        hop(2, 0, x_dn, x1[2])
        got(2, 0)
        yield
        for i, dz in enumerate((0, 1, -1, 2)):
            take(x1[dz], land.at[pl.ds(0, 2)])
            if i % 2:
                hop(dz, -1, x_dn, x2)
            else:
                hop(dz, 1, x_up, x2)
            got(dz, 1)
            got(dz, -1)
        yield
        take(x2, land.at[pl.ds(0, 4)])
        for dz in (0, 1, -1, 2):
            got(dz, 2)
        at_end.append(lambda: take(send, land.at[pl.ds(0, 15)]))
        yield

    def spread_a(j):
        send, recv, kept = new(), new(), new()

        def got(dz, dx):
            owner = chip_of(dz, dx)
            target = lax.rem(owner, 8)
            src, dst = a_ga[j].at[owner], a_all[j].at[lax.div(owner, 8), y]

            @pl.when(target != y)
            def _():
                remote(src, dst, at_ctx(zl * 8 + target), send, recv)

            @pl.when(target == y)
            def _():
                pltpu.make_async_copy(src, dst, kept).start()

        yield from gather(a_ga[j].at[chip], a_ga[j], j % 2 == 1, got)
        take(recv, a_ga[j].at[pl.ds(0, 14)])
        take(kept, a_ga[j].at[pl.ds(0, 2)])
        at_end.append(lambda: take(send, a_ga[j].at[pl.ds(0, 14)]))
        yield

    def spread_g(j):
        here = g_all[j].at[y]
        send, recv = new(), new()
        for peer in peers:
            remote(here, here, peer, send, recv)
        yield
        take(recv, g_all[j].at[pl.ds(0, 7)])
        at_end.append(lambda: take(send, g_all[j].at[pl.ds(0, 7)]))
        yield

    swaps = {}

    def rotate(q):
        v = (bi_v, bo_v)[q // n_chunks]
        if q % n_chunks == 0:
            own, other = b_copies[q // n_chunks]
            own.wait()
            other.wait_recv()
        own_copies[q].wait()
        n = CHUNKS[q % n_chunks][1]

        def add(s, total):
            return total + jnp.dot(x_land[q][s].reshape(2 * n, 256), v[s], preferred_element_type=F32)

        total = lax.fori_loop(0, CHIPS, add, jnp.zeros((2 * n, 256), F32))
        part[q][...] = total.reshape(2, n, 256)
        swaps[q] = swap(part[q].at[1 - core], part_in[q])

    def settle(q):
        j = q % n_chunks
        swaps[q].wait_recv()
        value = (part[q][core] + part_in[q][...]).astype(BF16)
        if q < n_chunks:
            a_ga[j][chip] = value
            gens["m", j] = spread_a(j)
        else:
            g_all[j][y] = value
            gens["g", j] = spread_g(j)

    gens = {("x", q): gather(shards[q], x_land[q], q % 2 == 1) for q in range(n_q)}
    for op, q in schedule(n_q):
        if op in "xmg":
            next(gens[op, q], None)
        elif op == "r":
            rotate(q)
        elif op == "s":
            settle(q)
        else:
            for copies, hbm, v in ((b_copies[0], bi_hbm, bi_v), (b_copies[1], bo_hbm, bo_v)):
                copies.append(swap(hbm.at[:, 1 - core], v.at[:, :, cols]))

    def multiply(j):
        n = CHUNKS[j][1]

        def add(i, _):
            some = pl.ds(i * 4, 4)
            left = g_all[j][some].reshape(4 * n, 256)
            for h in range(2):
                right = a_all[j][h, some].reshape(4 * n, 256)
                rot[h] += lax.dot_general(left, right, (((0,), (0,)), ((), ())), preferred_element_type=F32)
            return 0

        lax.fori_loop(0, 2, add, 0)

    rot[...] = jnp.zeros((2, 256, 256), F32)
    for j in range(n_chunks):
        multiply(j)
    halves = [pl.ds(pl.multiple_of((1 - core) * 128, 128), 128), pl.ds(pl.multiple_of(core * 128, 128), 128)]
    parts = [remote(rot.at[1 - zl, half], rot_in.at[half], over, new(), new()) for half in halves]
    at_end.extend(p.wait_send for p in parts)

    def square(i):
        parts[i].wait_recv()
        value = rot[zl, halves[i], :] + rot_in[halves[i], :]
        return value * value

    sq[...] = square(0)
    last = swap(sq, sq_in)
    mine = square(1)
    last.wait_recv()
    out_ref[...] = mine + sq_in[...]
    for finish in at_end:
        finish()


def body(out_grad, inputs, basis_out, basis_in, correction):
    tokens = out_grad.shape[0]
    half = tokens // GROUPS
    n_chunks = len(CHUNKS)
    sizes = [n for _, n in CHUNKS]
    scratch = [
        pltpu.VMEM((CHIPS, 256, 256), BF16),
        pltpu.VMEM((CHIPS, 256, 256), BF16),
        pltpu.VMEM((128, 256), F32),
        pltpu.VMEM((128, 256), F32),
        pltpu.VMEM((2, 256, 256), F32),
        pltpu.VMEM((256, 256), F32),
        pltpu.SemaphoreType.DMA((N_SEMS,)),
    ]
    scratch += [pltpu.VMEM((CHIPS, GROUPS, n, 256), BF16) for n in sizes * 2]
    scratch += [pltpu.VMEM((GROUPS, n, 256), F32) for n in sizes * 2]
    scratch += [pltpu.VMEM((n, 256), F32) for n in sizes * 2]
    scratch += [pltpu.VMEM((CHIPS, n, 256), BF16) for n in sizes]
    scratch += [pltpu.VMEM((2, 8, n, 256), BF16) for n in sizes]
    scratch += [pltpu.VMEM((8, n, 256), BF16) for n in sizes]
    squares = pl.pallas_call(
        kernel,
        name="ekfac",
        out_shape=jax.ShapeDtypeStruct(correction.shape, F32),
        in_specs=[pl.BlockSpec(memory_space=pl.ANY)] * 4,
        out_specs=pl.BlockSpec(memory_space=pltpu.VMEM),
        scratch_shapes=scratch,
        compiler_params=pltpu.CompilerParams(collective_id=0, has_side_effects=True, vmem_limit_bytes=62 << 20),
        cost_estimate=pl.CostEstimate(flops=3 * 10**9, bytes_accessed=5 * 10**6, transcendentals=0),
    )(
        out_grad.reshape(GROUPS, half, 256),
        inputs.reshape(GROUPS, half, 256),
        basis_out.reshape(CHIPS, 2, 256, 128),
        basis_in.reshape(CHIPS, 2, 256, 128),
    )
    return correction + squares / (tokens * lax.axis_size("ctx"))


def solution(mesh):
    return jax.shard_map(
        body,
        mesh=mesh,
        in_specs=(P("ctx", "basis"), P("ctx", "basis"), P(None, "basis"), P(None, "basis"), P("basis", "ctx")),
        out_specs=P("basis", "ctx"),
        check_vma=False,
    )
```

time: 321 us -> 107 us (0.33)
  the two profiles are of different devices: /device:TPU:6 before, /device:TPU:1 now
where the time goes in v2:
time: 107 us
  Pallas kernels  106 us (99%)
  other arithmetic  1.58 us (1%)
    pallas_call x1, Pallas kernels, body(): pl.pallas_call(kernel, name='ekfac', out_shape=jax.ShapeDtypeStruct(corre...  106 us

profile of v2, /device:TPU:1, one launch (start us, length us, event | category | flops | bytes accessed | tf_op | source)
XLA Modules:
  0.0 107.2 jit_solution(11189374095929763216)
XLA Ops:
  0.0 0.0 copy-start
  0.0 105.6 %ekfac.1 = f32[128,256]{1,0:T(8,128)} custom-call(bf16[2,144,256]{2,1,0:T(8,128)(2,1)} %bitcast.6, bf16[2,144,256]{2,1,0:T(8,128)(2,1)} %bitcast.7, bf16[16,2,256,128]{3,2,1,0:T(8,128)(2,1)} %bitcast.4, bf16[16,2,256,128]{3,2,1,0:T(8,128)(2,1)} %bitcast.5), custom_call_target="tpu_custom_call" | custom-call | flops 3000000000 | bytes 5000000 | tf_op jit(solution)/shard_map/ekfac/pallas_call | solution.py:310
  105.6 0.0 copy-done
  105.6 1.6 %multiply_add_fusion = f32[128,256]{1,0:T(8,128)} fusion(f32[128,256]{1,0:T(8,128)S(1)} %copy-done, f32[128,256]{1,0:T(8,128)} %ekfac.1), kind=kLoop, calls=%fused_computation | loop fusion | flops 65536 | bytes 393216 | tf_op jit(solution)/shard_map/add | solution.py:325
Async XLA Ops:
  0.0 105.6 %copy-start = (f32[128,256]{1,0:T(8,128)S(1)}, f32[128,256]{1,0:T(8,128)}, u32[]{:S(2)}) copy-start(f32[128,256]{1,0:T(8,128)} %param.9) | copy-start | bytes 393220

commit v3 on v2

--- a/solution.py
+++ b/solution.py
@@ -8,53 +8,25 @@
 MESH = pl.DeviceIdType.MESH
 GROUPS = 2
 CHIPS = 16
-CHUNKS = ((0, 80), (80, 64))
-N_SEMS = 90
+CHUNKS = (((0, 80), (80, 64)), ((0, 80), (80, 64)))
+ORDER = (
+    "x0", "x1", "x0", "x1", "b0", "x0", "x1", "x0", "x1", "x2", "x3", "x0", "x1", "x2", "x3", "x0",
+    "r0", "s0", "m0", "m0", "x1", "r1", "s1", "m1", "m1", "x2", "m0", "m1", "x2", "m0", "m1", "m0",
+    "m1", "x3", "x3", "x2", "m0", "m1", "x3", "x2", "r2", "s2", "g0", "g0", "x3", "r3", "s3", "g1",
+    "g0", "g0", "m0", "m1", "g0", "f0", "g1", "f1",
+)
+N_SEMS = 110
 F32 = jnp.float32
 BF16 = jnp.bfloat16
 
 
-def schedule(n):
-    h = n // 2
-    done = {}
-    steps = []
-
-    def add(op, q, upto=None):
-        if 0 <= q < (h if op in "mg" else n):
-            while upto is None or done.get((op, q), 0) < upto:
-                steps.append((op, q))
-                done[op, q] = done.get((op, q), 0) + 1
-                if upto is None:
-                    break
-
-    add("x", 0, 2)
-    add("x", 1, 1)
-    steps.append(("b", 0))
-    for q in range(n + 1):
-        add("x", q, 3)
-        add("x", q - 1, 6)
-        add("r", q - 1)
-        add("x", q, 4)
-        add("x", q + 1, 1)
-        add("m", q - 2, 3)
-        add("s", q - 1)
-        add("m", q - 1, 2)
-        add("g", q - 1 - h, 1)
-        add("m", q - 2, 4)
-        add("x", q, 5)
-        add("x", q + 1, 2)
-        add("m", q - 2, 6)
-        add("m", q - 1, 3)
-        add("g", q - 2 - h, 9)
-    return steps + [("m", j) for j in range(h) for _ in range(7 - done["m", j])] + [("g", j) for j in range(h) for _ in range(6)]
-
-
 def kernel(grad_hbm, in_hbm, bo_hbm, bi_hbm, out_ref, *scratch):
-    n_chunks = len(CHUNKS)
-    n_q = 2 * n_chunks
+    n_a, n_g = (len(c) for c in CHUNKS)
+    n_q = n_a + n_g
+    pieces = CHUNKS[0] + CHUNKS[1]
     (bo_v, bi_v, sq, sq_in, rot, rot_in, sems), rest = scratch[:7], scratch[7:]
     x_land, part, part_in = rest[:n_q], rest[n_q:2 * n_q], rest[2 * n_q:3 * n_q]
-    a_ga, a_all, g_all = (rest[3 * n_q + i * n_chunks:3 * n_q + (i + 1) * n_chunks] for i in range(3))
+    a_ga, g_mine, a_all, g_all = rest[3 * n_q:3 * n_q + n_a], rest[3 * n_q + n_a:4 * n_q], rest[4 * n_q], rest[4 * n_q + 1]
 
     ctx = lax.axis_index("ctx")
     basis = lax.axis_index("basis")
@@ -120,8 +92,7 @@
     b_copies = [[local(hbm.at[:, core], v.at[:, :, cols])] for hbm, v in ((bi_hbm, bi_v), (bo_hbm, bo_v))]
     shards, own_copies = [], []
     for q in range(n_q):
-        first, n = CHUNKS[q % n_chunks]
-        shards.append((in_hbm, grad_hbm)[q // n_chunks].at[:, pl.ds(first, n)])
+        shards.append((in_hbm if q < n_a else grad_hbm).at[:, pl.ds(*pieces[q])])
         own_copies.append(local(shards[q], x_land[q].at[chip]))
 
     pl.semaphore_wait(barrier, len(others))
@@ -186,7 +157,7 @@
         def got(dz, dx):
             owner = chip_of(dz, dx)
             target = lax.rem(owner, 8)
-            src, dst = a_ga[j].at[owner], a_all[j].at[lax.div(owner, 8), y]
+            src, dst = a_ga[j].at[owner], a_all.at[lax.div(owner, 8), y, pl.ds(*CHUNKS[0][j])]
 
             @pl.when(target != y)
             def _():
@@ -203,72 +174,99 @@
         yield
 
     def spread_g(j):
-        here = g_all[j].at[y]
-        send, recv = new(), new()
-        for peer in peers:
-            remote(here, here, peer, send, recv)
-        yield
-        take(recv, g_all[j].at[pl.ds(0, 7)])
-        at_end.append(lambda: take(send, g_all[j].at[pl.ds(0, 7)]))
+        rows = pl.ds(*CHUNKS[1][j])
+        here = g_all.at[y, rows]
+        send = new()
+        if j + 1 < n_g:
+            hops = [new() for _ in range(4)]
+            up, dn = peers[0], peers[6]
+
+            def hop(i):
+                above, below = (g_all.at[lax.rem(y + 8 + d, 8), rows] for d in (-i, i))
+                if i < 4:
+                    remote(above if i else g_mine[j], above, up, send, hops[i])
+                if i < 3:
+                    remote(below if i else g_mine[j], below, dn, send, hops[i])
+
+            hop(0)
+            yield
+            for i in range(1, 4):
+                take(hops[i - 1], g_all.at[pl.ds(0, 2), rows])
+                hop(i)
+                yield
+            take(hops[3], g_all.at[0, rows])
+        else:
+            recv = new()
+            for peer in peers:
+                remote(g_mine[j], here, peer, send, recv)
+            yield
+            take(recv, g_all.at[pl.ds(0, 7), rows])
+        at_end.append(lambda: take(send, g_all.at[pl.ds(0, 7), rows]))
         yield
 
     swaps = {}
 
     def rotate(q):
-        v = (bi_v, bo_v)[q // n_chunks]
-        if q % n_chunks == 0:
-            own, other = b_copies[q // n_chunks]
+        i = 0 if q < n_a else 1
+        v = (bi_v, bo_v)[i]
+        if q in (0, n_a):
+            own, other = b_copies[i]
             own.wait()
             other.wait_recv()
         own_copies[q].wait()
-        n = CHUNKS[q % n_chunks][1]
-
-        def add(s, total):
-            return total + jnp.dot(x_land[q][s].reshape(2 * n, 256), v[s], preferred_element_type=F32)
-
-        total = lax.fori_loop(0, CHIPS, add, jnp.zeros((2 * n, 256), F32))
+        n = pieces[q][1]
+
+        def add(i, total):
+            for s in range(4):
+                s += 4 * i
+                total += jnp.dot(x_land[q][s].reshape(2 * n, 256), v[s], preferred_element_type=F32)
+            return total
+
+        total = lax.fori_loop(0, CHIPS // 4, add, jnp.zeros((2 * n, 256), F32))
         part[q][...] = total.reshape(2, n, 256)
         swaps[q] = swap(part[q].at[1 - core], part_in[q])
 
     def settle(q):
-        j = q % n_chunks
         swaps[q].wait_recv()
         value = (part[q][core] + part_in[q][...]).astype(BF16)
-        if q < n_chunks:
-            a_ga[j][chip] = value
-            gens["m", j] = spread_a(j)
+        if q < n_a:
+            a_ga[q][chip] = value
+            gens["m", q] = spread_a(q)
         else:
-            g_all[j][y] = value
+            j = q - n_a
+            g_mine[j][...] = value
+            g_all[y, pl.ds(*pieces[q]), :] = value
             gens["g", j] = spread_g(j)
 
+    def multiply(j):
+        first, n = CHUNKS[1][j]
+        rows = pl.ds(first, n)
+
+        def add(i, _):
+            some = pl.ds(i * 4, 4)
+            left = g_all[some, rows, :].reshape(4 * n, 256)
+            for h in range(2):
+                right = a_all[h, some, rows, :].reshape(4 * n, 256)
+                rot[h] += lax.dot_general(left, right, (((0,), (0,)), ((), ())), preferred_element_type=F32)
+            return 0
+
+        lax.fori_loop(0, 2, add, 0)
+
     gens = {("x", q): gather(shards[q], x_land[q], q % 2 == 1) for q in range(n_q)}
-    for op, q in schedule(n_q):
+    rot[...] = jnp.zeros((2, 256, 256), F32)
+    for step in ORDER:
+        op, q = step[0], int(step[1])
         if op in "xmg":
-            next(gens[op, q], None)
+            next(gens[op, q])
         elif op == "r":
             rotate(q)
         elif op == "s":
             settle(q)
+        elif op == "f":
+            multiply(q)
         else:
             for copies, hbm, v in ((b_copies[0], bi_hbm, bi_v), (b_copies[1], bo_hbm, bo_v)):
                 copies.append(swap(hbm.at[:, 1 - core], v.at[:, :, cols]))
-
-    def multiply(j):
-        n = CHUNKS[j][1]
-
-        def add(i, _):
-            some = pl.ds(i * 4, 4)
-            left = g_all[j][some].reshape(4 * n, 256)
-            for h in range(2):
-                right = a_all[j][h, some].reshape(4 * n, 256)
-                rot[h] += lax.dot_general(left, right, (((0,), (0,)), ((), ())), preferred_element_type=F32)
-            return 0
-
-        lax.fori_loop(0, 2, add, 0)
-
-    rot[...] = jnp.zeros((2, 256, 256), F32)
-    for j in range(n_chunks):
-        multiply(j)
     halves = [pl.ds(pl.multiple_of((1 - core) * 128, 128), 128), pl.ds(pl.multiple_of(core * 128, 128), 128)]
     parts = [remote(rot.at[1 - zl, half], rot_in.at[half], over, new(), new()) for half in halves]
     at_end.extend(p.wait_send for p in parts)
@@ -290,8 +288,8 @@
 def body(out_grad, inputs, basis_out, basis_in, correction):
     tokens = out_grad.shape[0]
     half = tokens // GROUPS
-    n_chunks = len(CHUNKS)
-    sizes = [n for _, n in CHUNKS]
+    sizes = [[n for _, n in c] for c in CHUNKS]
+    both = sizes[0] + sizes[1]
     scratch = [
         pltpu.VMEM((CHIPS, 256, 256), BF16),
         pltpu.VMEM((CHIPS, 256, 256), BF16),
@@ -301,12 +299,12 @@
         pltpu.VMEM((256, 256), F32),
         pltpu.SemaphoreType.DMA((N_SEMS,)),
     ]
-    scratch += [pltpu.VMEM((CHIPS, GROUPS, n, 256), BF16) for n in sizes * 2]
-    scratch += [pltpu.VMEM((GROUPS, n, 256), F32) for n in sizes * 2]
-    scratch += [pltpu.VMEM((n, 256), F32) for n in sizes * 2]
-    scratch += [pltpu.VMEM((CHIPS, n, 256), BF16) for n in sizes]
-    scratch += [pltpu.VMEM((2, 8, n, 256), BF16) for n in sizes]
-    scratch += [pltpu.VMEM((8, n, 256), BF16) for n in sizes]
+    scratch += [pltpu.VMEM((CHIPS, GROUPS, n, 256), BF16) for n in both]
+    scratch += [pltpu.VMEM((GROUPS, n, 256), F32) for n in both]
+    scratch += [pltpu.VMEM((n, 256), F32) for n in both]
+    scratch += [pltpu.VMEM((CHIPS, n, 256), BF16) for n in sizes[0]]
+    scratch += [pltpu.VMEM((n, 256), BF16) for n in sizes[1]]
+    scratch += [pltpu.VMEM((2, 8, half, 256), BF16), pltpu.VMEM((8, half, 256), BF16)]
     squares = pl.pallas_call(
         kernel,
         name="ekfac",

time: 107 us -> 103 us (0.963)
  Pallas kernels: 106 us -> 101 us
    pallas_call x1, Pallas kernels: 106 us -> 101 us  [body(): pl.pallas_call(kernel, name='ekfac', out_shape=jax.ShapeDtypeStruct(corre...]
where the time goes in v3:
time: 103 us; the launch traced here: 102 us
  Pallas kernels  101 us (98%)
  other arithmetic  1.58 us (2%)
    pallas_call x1, Pallas kernels, body(): pl.pallas_call(kernel, name='ekfac', out_shape=jax.ShapeDtypeStruct(corre...  101 us

profile of v3, /device:TPU:1, one launch (start us, length us, event | category | flops | bytes accessed | tf_op | source)
XLA Modules:
  0.0 102.4 jit_solution(16568759759908946363)
XLA Ops:
  0.0 0.0 copy-start
  0.0 100.8 %ekfac.1 = f32[128,256]{1,0:T(8,128)} custom-call(bf16[2,144,256]{2,1,0:T(8,128)(2,1)} %bitcast.6, bf16[2,144,256]{2,1,0:T(8,128)(2,1)} %bitcast.7, bf16[16,2,256,128]{3,2,1,0:T(8,128)(2,1)} %bitcast.4, bf16[16,2,256,128]{3,2,1,0:T(8,128)(2,1)} %bitcast.5), custom_call_target="tpu_custom_call" | custom-call | flops 3000000000 | bytes 5000000 | tf_op jit(solution)/shard_map/ekfac/pallas_call | solution.py:308
  100.8 0.0 copy-done
  100.9 1.6 %multiply_add_fusion = f32[128,256]{1,0:T(8,128)} fusion(f32[128,256]{1,0:T(8,128)S(1)} %copy-done, f32[128,256]{1,0:T(8,128)} %ekfac.1), kind=kLoop, calls=%fused_computation | loop fusion | flops 65536 | bytes 393216 | tf_op jit(solution)/shard_map/add | solution.py:323
Async XLA Ops:
  0.0 100.8 %copy-start = (f32[128,256]{1,0:T(8,128)S(1)}, f32[128,256]{1,0:T(8,128)}, u32[]{:S(2)}) copy-start(f32[128,256]{1,0:T(8,128)} %param.9) | copy-start | bytes 393220

commit v4 on v3

--- a/solution.py
+++ b/solution.py
@@ -10,12 +10,12 @@
 CHIPS = 16
 CHUNKS = (((0, 80), (80, 64)), ((0, 80), (80, 64)))
 ORDER = (
-    "x0", "x1", "x0", "x1", "b0", "x0", "x1", "x0", "x1", "x2", "x3", "x0", "x1", "x2", "x3", "x0",
-    "r0", "s0", "m0", "m0", "x1", "r1", "s1", "m1", "m1", "x2", "m0", "m1", "x2", "m0", "m1", "m0",
-    "m1", "x3", "x3", "x2", "m0", "m1", "x3", "x2", "r2", "s2", "g0", "g0", "x3", "r3", "s3", "g1",
-    "g0", "g0", "m0", "m1", "g0", "f0", "g1", "f1",
+    "x0", "x1", "x0", "x1", "b0", "x0", "x1", "x0", "x1", "x0", "x1", "x2", "x3", "x0", "r0", "x1",
+    "r1", "s0", "m0", "m0", "s1", "m1", "m1", "x2", "x3", "m0", "m1", "m0", "m1", "m0", "m1", "x2",
+    "x3", "x2", "x3", "m0", "m1", "x2", "x3", "x2", "r2", "s2", "g0", "x3", "r3", "g0", "s3", "g1",
+    "g0", "g0", "m0", "m1", "g0", "f0", "g1",
 )
-N_SEMS = 110
+N_SEMS = 85
 F32 = jnp.float32
 BF16 = jnp.bfloat16
 
@@ -238,14 +238,14 @@
             g_all[y, pl.ds(*pieces[q]), :] = value
             gens["g", j] = spread_g(j)
 
-    def multiply(j):
+    def multiply(j, tiles):
         first, n = CHUNKS[1][j]
         rows = pl.ds(first, n)
 
         def add(i, _):
             some = pl.ds(i * 4, 4)
             left = g_all[some, rows, :].reshape(4 * n, 256)
-            for h in range(2):
+            for h in tiles:
                 right = a_all[h, some, rows, :].reshape(4 * n, 256)
                 rot[h] += lax.dot_general(left, right, (((0,), (0,)), ((), ())), preferred_element_type=F32)
             return 0
@@ -263,13 +263,15 @@
         elif op == "s":
             settle(q)
         elif op == "f":
-            multiply(q)
+            multiply(q, (0, 1))
         else:
             for copies, hbm, v in ((b_copies[0], bi_hbm, bi_v), (b_copies[1], bo_hbm, bo_v)):
                 copies.append(swap(hbm.at[:, 1 - core], v.at[:, :, cols]))
+    multiply(n_g - 1, (1 - zl,))
     halves = [pl.ds(pl.multiple_of((1 - core) * 128, 128), 128), pl.ds(pl.multiple_of(core * 128, 128), 128)]
     parts = [remote(rot.at[1 - zl, half], rot_in.at[half], over, new(), new()) for half in halves]
     at_end.extend(p.wait_send for p in parts)
+    multiply(n_g - 1, (zl,))
 
     def square(i):
         parts[i].wait_recv()
@@ -283,6 +285,7 @@
     out_ref[...] = mine + sq_in[...]
     for finish in at_end:
         finish()
+    assert used[0] == N_SEMS, used[0]
 
 
 def body(out_grad, inputs, basis_out, basis_in, correction):

time: 103 us -> 102 us (level)
  no operation moved by 1% of the time
where the time goes in v4:
time: 102 us
  Pallas kernels  100 us (98%)
  other arithmetic  1.58 us (2%)
    pallas_call x1, Pallas kernels, body(): pl.pallas_call(kernel, name='ekfac', out_shape=jax.ShapeDtypeStruct(corre...  100 us

profile of v4, /device:TPU:1, one launch (start us, length us, event | category | flops | bytes accessed | tf_op | source)
XLA Modules:
  0.0 101.7 jit_solution(11266385026481076738)
XLA Ops:
  0.0 0.0 copy-start
  0.0 100.1 %ekfac.1 = f32[128,256]{1,0:T(8,128)} custom-call(bf16[2,144,256]{2,1,0:T(8,128)(2,1)} %bitcast.6, bf16[2,144,256]{2,1,0:T(8,128)(2,1)} %bitcast.7, bf16[16,2,256,128]{3,2,1,0:T(8,128)(2,1)} %bitcast.4, bf16[16,2,256,128]{3,2,1,0:T(8,128)(2,1)} %bitcast.5), custom_call_target="tpu_custom_call" | custom-call | flops 3000000000 | bytes 5000000 | tf_op jit(solution)/shard_map/ekfac/pallas_call | solution.py:311
  100.1 0.0 copy-done
  100.1 1.6 %multiply_add_fusion = f32[128,256]{1,0:T(8,128)} fusion(f32[128,256]{1,0:T(8,128)S(1)} %copy-done, f32[128,256]{1,0:T(8,128)} %ekfac.1), kind=kLoop, calls=%fused_computation | loop fusion | flops 65536 | bytes 393216 | tf_op jit(solution)/shard_map/add | solution.py:326
Async XLA Ops:
  0.0 100.1 %copy-start = (f32[128,256]{1,0:T(8,128)S(1)}, f32[128,256]{1,0:T(8,128)}, u32[]{:S(2)}) copy-start(f32[128,256]{1,0:T(8,128)} %param.9) | copy-start | bytes 393220

commit v5 on v4

--- a/solution.py
+++ b/solution.py
@@ -12,7 +12,7 @@
 ORDER = (
     "x0", "x1", "x0", "x1", "b0", "x0", "x1", "x0", "x1", "x0", "x1", "x2", "x3", "x0", "r0", "x1",
     "r1", "s0", "m0", "m0", "s1", "m1", "m1", "x2", "x3", "m0", "m1", "m0", "m1", "m0", "m1", "x2",
-    "x3", "x2", "x3", "m0", "m1", "x2", "x3", "x2", "r2", "s2", "g0", "x3", "r3", "g0", "s3", "g1",
+    "x3", "x2", "x3", "m0", "m1", "x2", "x3", "x2", "r2", "x3", "s2", "g0", "r3", "g0", "s3", "g1",
     "g0", "g0", "m0", "m1", "g0", "f0", "g1",
 )
 N_SEMS = 85

time: 102 us -> 102 us (level)
  no operation moved by 1% of the time
where the time goes in v5:
time: 102 us
  Pallas kernels  100 us (98%)
  other arithmetic  1.58 us (2%)
    pallas_call x1, Pallas kernels, body(): pl.pallas_call(kernel, name='ekfac', out_shape=jax.ShapeDtypeStruct(corre...  100 us

profile of v5, /device:TPU:1, one launch (start us, length us, event | category | flops | bytes accessed | tf_op | source)
XLA Modules:
  0.0 101.9 jit_solution(1197461847714060940)
XLA Ops:
  0.0 0.0 copy-start
  0.0 100.3 %ekfac.1 = f32[128,256]{1,0:T(8,128)} custom-call(bf16[2,144,256]{2,1,0:T(8,128)(2,1)} %bitcast.6, bf16[2,144,256]{2,1,0:T(8,128)(2,1)} %bitcast.7, bf16[16,2,256,128]{3,2,1,0:T(8,128)(2,1)} %bitcast.4, bf16[16,2,256,128]{3,2,1,0:T(8,128)(2,1)} %bitcast.5), custom_call_target="tpu_custom_call" | custom-call | flops 3000000000 | bytes 5000000 | tf_op jit(solution)/shard_map/ekfac/pallas_call | solution.py:311
  100.3 0.0 copy-done
  100.3 1.6 %multiply_add_fusion = f32[128,256]{1,0:T(8,128)} fusion(f32[128,256]{1,0:T(8,128)S(1)} %copy-done, f32[128,256]{1,0:T(8,128)} %ekfac.1), kind=kLoop, calls=%fused_computation | loop fusion | flops 65536 | bytes 393216 | tf_op jit(solution)/shard_map/add | solution.py:326
Async XLA Ops:
  0.0 100.3 %copy-start = (f32[128,256]{1,0:T(8,128)S(1)}, f32[128,256]{1,0:T(8,128)}, u32[]{:S(2)}) copy-start(f32[128,256]{1,0:T(8,128)} %param.9) | copy-start | bytes 393220

commit v6 on v4

--- a/solution.py
+++ b/solution.py
@@ -197,8 +197,8 @@
             take(hops[3], g_all.at[0, rows])
         else:
             recv = new()
-            for peer in peers:
-                remote(g_mine[j], here, peer, send, recv)
+            for i in (3, 2, 4, 1, 5, 0, 6):
+                remote(g_mine[j], here, peers[i], send, recv)
             yield
             take(recv, g_all.at[pl.ds(0, 7), rows])
         at_end.append(lambda: take(send, g_all.at[pl.ds(0, 7), rows]))

time: 102 us -> 101 us (level)
  no operation moved by 1% of the time
where the time goes in v6:
time: 101 us
  Pallas kernels  99.2 us (98%)
  other arithmetic  1.58 us (2%)
    pallas_call x1, Pallas kernels, body(): pl.pallas_call(kernel, name='ekfac', out_shape=jax.ShapeDtypeStruct(corre...  99.2 us

profile of v6, /device:TPU:1, one launch (start us, length us, event | category | flops | bytes accessed | tf_op | source)
XLA Modules:
  0.0 100.8 jit_solution(10605279521677268173)
XLA Ops:
  0.0 0.0 copy-start
  0.0 99.2 %ekfac.1 = f32[128,256]{1,0:T(8,128)} custom-call(bf16[2,144,256]{2,1,0:T(8,128)(2,1)} %bitcast.6, bf16[2,144,256]{2,1,0:T(8,128)(2,1)} %bitcast.7, bf16[16,2,256,128]{3,2,1,0:T(8,128)(2,1)} %bitcast.4, bf16[16,2,256,128]{3,2,1,0:T(8,128)(2,1)} %bitcast.5), custom_call_target="tpu_custom_call" | custom-call | flops 3000000000 | bytes 5000000 | tf_op jit(solution)/shard_map/ekfac/pallas_call | solution.py:311
  99.2 0.0 copy-done
  99.2 1.6 %multiply_add_fusion = f32[128,256]{1,0:T(8,128)} fusion(f32[128,256]{1,0:T(8,128)S(1)} %copy-done, f32[128,256]{1,0:T(8,128)} %ekfac.1), kind=kLoop, calls=%fused_computation | loop fusion | flops 65536 | bytes 393216 | tf_op jit(solution)/shard_map/add | solution.py:326
Async XLA Ops:
  0.0 99.2 %copy-start = (f32[128,256]{1,0:T(8,128)S(1)}, f32[128,256]{1,0:T(8,128)}, u32[]{:S(2)}) copy-start(f32[128,256]{1,0:T(8,128)} %param.9) | copy-start | bytes 393220
